TPU v7x, 128 devices: a whole 4x4x4 slice. The times are simulated.
128 devices in a mesh: section: 8 (over x, core), expert: 16 (over y, z).
Axes of the slice: x: 4, y: 4, z: 4, core: 2. Of those that a mesh axis runs over, the one named last changes fastest.
Arguments:
- arriving: bfloat16 [16384, 2560], P(('section', 'expert')), may hold values from -6 to 6
- expert_id: int32 [16384, 1], P(('section', 'expert')), may hold values from 0 to 15; in each aligned block of 128 rows (0 to 127, 128 to 255, ...) at most 10 rows name the same one
- router: bfloat16 [2560, 16], replicated, may hold values from -0.125 to 0.125
- gate_weight: bfloat16 [16, 2560, 6144], P('expert', None, 'section'), may hold values from -0.125 to 0.125
- up_weight: bfloat16 [16, 2560, 6144], P('expert', None, 'section'), may hold values from -0.125 to 0.125
- down_weight: bfloat16 [16, 6144, 2560], P('expert', 'section'), may hold values from -0.078125 to 0.078125
- shared_gate: bfloat16 [2560, 6144], P(None, 'section'), may hold values from -0.125 to 0.125
- shared_up: bfloat16 [2560, 6144], P(None, 'section'), may hold values from -0.125 to 0.125
- shared_down: bfloat16 [6144, 2560], P('section'), may hold values from -0.078125 to 0.078125
Outputs:
- mixed: bfloat16 [16384, 2560], P(('section', 'expert'))
Inputs may be any that keep to these rules, and one draw needn't show every extreme that they name: `expert_id`: among the 128 rows of one device no expert is named more than 10 times, and in every draw some expert is named exactly 10 times by the rows of some device; every expert is named by some row.
All inputs are finite; a program needn't handle non-finite values.
Results may differ from a plain program's by a relative error of at most 0.0049.
Values may be sent and summed in bfloat16 or wider, within the bound.
A program may use at most 192 MiB of HBM per device.

v0:
```python
import jax
import jax.numpy as jnp
from jax import lax
from jax.sharding import PartitionSpec as P


def passed_along(value, axis, steps):
    count = lax.axis_size(axis)
    pairs = [(source, (source + steps) % count) for source in range(count)]
    return lax.ppermute(value, axis, pairs)


def swiglu(row_block, gate_mat, up_mat):
    gate_part = jnp.dot(row_block, gate_mat, preferred_element_type=jnp.float32)
    up_part = jnp.dot(row_block, up_mat, preferred_element_type=jnp.float32)
    return (jax.nn.silu(gate_part) * up_part).astype(jnp.bfloat16)


def on_device(
    arriving,
    expert_id,
    router,
    gate_weight,
    up_weight,
    down_weight,
    shared_gate,
    shared_up,
    shared_down,
):
    tokens = passed_along(arriving, "section", 1)
    tok_rows = tokens.shape[0]
    model_width = tokens.shape[1]
    experts = router.shape[1]
    capacity = 5 * tok_rows // (4 * experts)
    slot_count = experts * capacity
    chosen = expert_id[:, 0]
    onehot = (chosen[:, None] == jnp.arange(experts, dtype=jnp.int32)[None, :]).astype(jnp.int32)
    before = jnp.cumsum(onehot, axis=0, dtype=jnp.int32) - onehot
    rank_in = jnp.sum(before * onehot, axis=1, dtype=jnp.int32)
    slot_index = chosen * capacity + rank_in
    outgoing = jnp.zeros((slot_count, model_width), tokens.dtype).at[slot_index].set(tokens)
    incoming = lax.all_to_all(
        outgoing.reshape(experts, capacity, model_width),
        "expert",
        split_axis=0,
        concat_axis=0,
        tiled=True,
    )
    slot_rows_here = incoming.reshape(slot_count, model_width)
    column = lax.dynamic_slice_in_dim(router, lax.axis_index("expert"), 1, 1)
    gate_local = gate_weight[0]
    up_local = up_weight[0]
    down_local = down_weight[0]
    all_slots, all_home = (
        lax.all_gather(slot_rows_here, "section", axis=0, tiled=True),
        lax.all_gather(tokens, "section", axis=0, tiled=True),
    )
    routed_hidden = swiglu(all_slots, gate_local, up_local)
    shared_hidden = swiglu(all_home, shared_gate, shared_up)
    gate_prob = jax.nn.sigmoid(jnp.dot(all_slots, column, preferred_element_type=jnp.float32))
    group_rows = slot_count + tok_rows
    groups = lax.axis_size("section") * group_rows // group_rows
    routed = jnp.dot(routed_hidden, down_local, preferred_element_type=jnp.float32) * gate_prob
    shared = jnp.dot(shared_hidden, shared_down, preferred_element_type=jnp.float32)
    joined = jnp.concatenate(
        [
            routed.reshape(groups, slot_count, model_width),
            shared.reshape(groups, tok_rows, model_width),
        ],
        axis=1,
    )
    summed = lax.psum_scatter(
        joined.reshape(lax.axis_size("section") * group_rows, model_width),
        "section",
        scatter_dimension=0,
        tiled=True,
    )
    returned = lax.all_to_all(
        summed[:slot_count].reshape(experts, capacity, model_width),
        "expert",
        split_axis=0,
        concat_axis=0,
        tiled=True,
    )
    routed_home = jnp.take(returned.reshape(slot_count, model_width), slot_index, axis=0)
    mixed_out = summed[slot_count:] + routed_home
    return mixed_out.astype(jnp.bfloat16)


def solution(mesh):
    placed = (
        P(("section", "expert"), None),
        P(("section", "expert"), None),
        P(),
        P("expert", None, "section"),
        P("expert", None, "section"),
        P("expert", "section", None),
        P(None, "section"),
        P(None, "section"),
        P("section", None),
    )
    return jax.shard_map(
        on_device,
        mesh=mesh,
        in_specs=placed,
        out_specs=P(("section", "expert"), None),
        check_vma=False,
    )
```

profile of v0, /device:TPU:1, one launch (start us, length us, event | category | flops | bytes accessed | tf_op | source)
XLA Modules:
  0.0 330.5 jit_solution(7314631868801470495)
XLA Ops:
  6.5 0.0 copy-start
  6.5 0.0 all-gather.5.cloned.1.call-start
  6.5 2.6 collective-permute-start
  9.1 7.8 %collective-permute-done = bf16[128,2560]{1,0:T(8,128)(2,1)S(1)} collective-permute-done((bf16[128,2560]{1,0:T(8,128)(2,1)}, bf16[128,2560]{1,0:T(8,128)(2,1)S(1)}, u32[]{:S(2)}, u32[]{:S(2)}) %collective-permute-start) | collective-permute-done | bytes 655392 | tf_op jit(solution)/shard_map/ppermute | solution.py:10
  17.0 0.0 copy-start.3
  17.0 0.8 copy-done.3
  17.8 0.0 all-gather.5.cloned.1.call-update
  17.8 0.0 all-gather.3.cloned.1.call-start
  17.9 0.7 fusion.14
  18.6 0.2 reduce_window_sum.11
  18.8 0.8 select_reduce_fusion
  19.6 0.7 and_bitcast_fusion
  20.3 2.3 scatter_custom_fusion
  22.6 0.3 reshape.36
  23.0 24.0 %all_to_all.10 = bf16[16,10,2560]{2,1,0:T(8,128)(2,1)S(1)} all-to-all(bf16[16,10,2560]{2,1,0:T(8,128)(2,1)S(1)} %reshape.36), channel_id=1, replica_groups=mesh['section'=8,'expert'=16] {'expert'}, dimensions={0} | all-to-all | bytes 1638400 | tf_op jit(solution)/shard_map/all_to_all | solution.py:42
  47.0 1.1 reshape.37
  48.1 0.0 all-gather.3.cloned.1.call-update
  48.1 0.2 reduce-scatter.2.cloned.1.call-start
  48.3 9.5 %all-gather.5.cloned.1.call-done = bf16[1024,2560]{1,0:T(8,128)(2,1)} async-done(((bf16[128,2560]{1,0:T(8,128)(2,1)}), bf16[1024,2560]{1,0:T(8,128)(2,1)}) %all-gather.5.cloned.1.call-update) | async-done | bytes 5242896 | tf_op jit(solution)/shard_map/all_gather | solution.py:56
  57.9 7.3 %fusion.21 = f32[1024,768]{1,0:T(8,128)S(1)} fusion(bf16[1024,2560]{1,0:T(8,128)(2,1)} %all-gather.5.cloned.1.call-done, bf16[2560,768]{1,0:T(8,128)(2,1)} %param.15), kind=kOutput, calls=%fused_computation.31 | convolution fusion | flops 4026531840 | bytes 12320768 | tf_op jit(solution)/shard_map/dot_general | solution.py:14
  65.2 17.9 %fusion.7 = f32[1024,2560]{1,0:T(8,128)} fusion(bf16[768,2560]{1,0:T(8,128)(2,1)} %param.17, f32[1024,768]{1,0:T(8,128)S(1)} %fusion.21, bf16[1024,2560]{1,0:T(8,128)(2,1)} %all-gather.5.cloned.1.call-done, bf16[2560,768]{1,0:T(8,128)(2,1)} %param.16), kind=kOutput, calls=%fused_computation.11 | convolution fusion | flops 8057782272 | bytes 26738688 | tf_op jit(solution)/shard_map/dot_general | solution.py:64
  83.1 18.5 %all-gather.3.cloned.1.call-done = bf16[1280,2560]{1,0:T(8,128)(2,1)} async-done(((bf16[160,2560]{1,0:T(8,128)(2,1)}), bf16[1280,2560]{1,0:T(8,128)(2,1)}) %all-gather.3.cloned.1.call-update) | async-done | bytes 6553616 | tf_op jit(solution)/shard_map/all_gather | solution.py:55
  101.6 0.0 copy-done
  101.6 0.0 copy-start.2
  101.6 4.8 %convolution_reduce_fusion = f32[1280]{0:T(1024)S(1)} fusion(bf16[1280,2560]{1,0:T(8,128)(2,1)} %all-gather.3.cloned.1.call-done, bf16[2560,16]{0,1:T(8,128)(2,1)S(1)} %copy-done, s32[]{:T(128)S(6)} %select_n.16), kind=kOutput, calls=%fused_computation.15 | convolution fusion | flops 6553600 | bytes 6568964 | tf_op jit(solution)/shard_map/dot_general | solution.py:60
  106.5 0.0 copy-done.2
  106.5 9.3 %fusion.2 = f32[1280,768]{1,0:T(8,128)} fusion(bf16[1280,2560]{1,0:T(8,128)(2,1)S(1)} %copy-done.2, bf16[1,2560,768]{2,1,0:T(8,128)(2,1)} %param.12), kind=kOutput, calls=%fused_computation.7 | convolution fusion | flops 5033164800 | bytes 14417920 | tf_op jit(solution)/shard_map/dot_general | solution.py:14
  115.8 21.3 %convolution_multiply_fusion = f32[1280,2560]{1,0:T(8,128)} fusion(f32[1280]{0:T(1024)S(1)} %add_divide_fusion, bf16[1,768,2560]{2,1,0:T(8,128)(2,1)} %param.14, bf16[1280,2560]{1,0:T(8,128)(2,1)} %all-gather.3.cloned.1.call-done, bf16[1,2560,768]{2,1,0:T(8,128)(2,1)} %param.13, f32[1280,768]{1,0:T(8,128)} %fusion.2), kind=kOutput, calls=%fused_computation.3 | convolution fusion | flops 10075504640 | bytes 31462400 | tf_op jit(solution)/shard_map/dot_general | solution.py:63
  137.1 16.3 %pad_maximum_fusion = f32[8,288,2560]{2,1,0:T(8,128)} fusion(f32[8,128,2560]{2,1,0:T(8,128)} %bitcast.35, f32[8,160,2560]{2,1,0:T(8,128)} %bitcast.34), kind=kLoop, calls=%fused_computation.2 | loop fusion | flops 5898240 | bytes 47185920 | tf_op jit(solution)/shard_map/concatenate | solution.py:65
  153.4 0.0 reduce-scatter.2.cloned.1.call-update
  153.4 123.2 %reduce-scatter.2.cloned.1.call-done = f32[288,2560]{1,0:T(8,128)} async-done(((f32[2304,2560]{1,0:T(8,128)}), f32[288,2560]{1,0:T(8,128)}) %reduce-scatter.2.cloned.1.call-update) | async-done | bytes 2949136 | tf_op jit(solution)/shard_map/reduce_scatter | solution.py:72
  276.6 0.0 slice-start
  276.6 1.4 slice-done
  278.0 1.6 reshape.42
  279.7 6.7 %all-to-all-start.1 = ((f32[16,10,2560]{2,1,0:T(8,128)}), f32[16,10,2560]{2,1,0:T(8,128)}, u32[]{:S(2)}, u32[]{:S(2)}) async-start(f32[16,10,2560]{2,1,0:T(8,128)} %reshape.42), calls=%async_computation.2 | async-start | bytes 5242880 | tf_op jit(solution)/shard_map/all_to_all | solution.py:78
  286.4 32.2 %all-to-all-done.1 = f32[16,10,2560]{2,1,0:T(8,128)} async-done(((f32[16,10,2560]{2,1,0:T(8,128)}), f32[16,10,2560]{2,1,0:T(8,128)}, u32[]{:S(2)}, u32[]{:S(2)}) %all-to-all-start.1) | async-done | bytes 1638432 | tf_op jit(solution)/shard_map/all_to_all | solution.py:78
  318.6 1.8 reshape.43
  320.5 0.0 copy-start.1
  320.5 1.1 gather_fusion
  321.6 2.3 fusion.11
  323.9 0.0 copy-done.1
  (2 shorter events, 0.0 us)
Async XLA Ops:
  6.5 95.1 %copy-start = (bf16[2560,16]{0,1:T(8,128)(2,1)S(1)}, bf16[2560,16]{0,1:T(8,128)(2,1)}, u32[]{:S(2)}) copy-start(bf16[2560,16]{0,1:T(8,128)(2,1)} %param.11) | copy-start | bytes 245764
  6.5 51.3 %all-gather.5.cloned.1.call-start = ((), (), s32[]{:S(2)}) async-start(), calls=%async_computation.4 | async-start | bytes 5898240 | tf_op jit(solution)/shard_map/all_gather | solution.py:56
  6.5 10.4 %collective-permute-start = (bf16[128,2560]{1,0:T(8,128)(2,1)}, bf16[128,2560]{1,0:T(8,128)(2,1)S(1)}, u32[]{:S(2)}, u32[]{:S(2)}) collective-permute-start(bf16[128,2560]{1,0:T(8,128)(2,1)} %param.9), channel_id=1, source_target_pairs={{0,16},{16,32},{32,48},{48,64},{64,80},{80,96},{96,112},{112,0},{1... | collective-permute-start | bytes 1966088 | tf_op jit(solution)/shard_map/ppermute | solution.py:10
  17.0 0.8 copy-start.3
  17.8 83.8 %all-gather.3.cloned.1.call-start = ((), (), s32[]{:S(2)}) async-start(), calls=%async_computation.3 | async-start | bytes 7372800 | tf_op jit(solution)/shard_map/all_gather | solution.py:55
  48.1 228.5 %reduce-scatter.2.cloned.1.call-start = ((), (), s32[]{:S(2)}) async-start(), calls=%async_computation.5 | async-start | bytes 26542080 | tf_op jit(solution)/shard_map/reduce_scatter | solution.py:72
  101.6 4.8 %copy-start.2 = (bf16[1280,2560]{1,0:T(8,128)(2,1)S(1)}, bf16[1280,2560]{1,0:T(8,128)(2,1)}, u32[]{:S(2)}) copy-start(bf16[1280,2560]{1,0:T(8,128)(2,1)} %all-gather.3.cloned.1.call-done) | copy-start | bytes 19660804
  276.6 1.4 slice-start
  279.7 39.0 %all-to-all-start.1 = ((f32[16,10,2560]{2,1,0:T(8,128)}), f32[16,10,2560]{2,1,0:T(8,128)}, u32[]{:S(2)}, u32[]{:S(2)}) async-start(f32[16,10,2560]{2,1,0:T(8,128)} %reshape.42), calls=%async_computation.2 | async-start | bytes 5242880 | tf_op jit(solution)/shard_map/all_to_all | solution.py:78
  320.5 3.4 %copy-start.1 = (bf16[2560,16]{0,1:T(8,128)(2,1)S(1)}, bf16[2560,16]{0,1:T(8,128)(2,1)}, u32[]{:S(2)}) copy-start(bf16[2560,16]{0,1:T(8,128)(2,1)} %param.11) | copy-start | bytes 245764
Sparse Core Ops, SparseCore 0:
  18.0 39.8 all-gather.4
  59.6 41.9 all-gather.2
  153.6 123.0 reduce-scatter.1
where the time goes:
time: 336 us; the launch traced here: 330 us
  waiting for transfers between devices  191 us (57%)
  matrix products  60.6 us (18%)
  blocking collectives  24 us (7%)
  other arithmetic  21.1 us (6%)
  between operations  13.2 us (4%)
  local copies, waits for them, and re-layouts  10.5 us (3%)
  starting transfers between devices  9.61 us (3%)
    reduce_scatter x1, waiting for transfers between devices, on_device(): lax.psum_scatter(joined.reshape(lax.axis_size('section') * group_rows, mo...  123 us
    all_to_all x1, waiting for transfers between devices, on_device(): lax.all_to_all(summed[:slot_count].reshape(experts, capacity, model_width...  32.2 us
    all_to_all x1, blocking collectives, on_device(): lax.all_to_all(outgoing.reshape(experts, capacity, model_width), 'expert'...  24 us
    dot_general x1, matrix products, on_device(): jnp.dot(routed_hidden, down_local, preferred_element_type=jnp.float32)  21.3 us
    all_gather x1, waiting for transfers between devices, on_device(): lax.all_gather(slot_rows_here, 'section', axis=0, tiled=True)  18.5 us
    dot_general x1, matrix products, on_device(): jnp.dot(shared_hidden, shared_down, preferred_element_type=jnp.float32)  17.9 us
    dot_general x2, matrix products, swiglu(): gate_part = jnp.dot(row_block, gate_mat, preferred_element_type=jnp.float32)  16.6 us
    concatenate x1, other arithmetic, on_device(): jnp.concatenate([routed.reshape(groups, slot_count, model_width), shared....  16.3 us
  transfers between devices with their start and end apart: 5, of which 5 were waited for; matrix products, arithmetic and copies ran while one was open for 9% of the time, Pallas kernels for 0%

commit v1 on v0

v1 whole, which is shorter than its diff:
```python
import jax
import jax.numpy as jnp
from jax import lax
from jax.experimental import pallas as pl
from jax.experimental.pallas import tpu as pltpu
from jax.sharding import PartitionSpec as P

MESH = pl.DeviceIdType.MESH
F32 = jnp.float32
BF16 = jnp.bfloat16

SECTIONS = 8
EXPERTS = 16
TOK = 128
CAP = 10
GROUP = 16
SLOTS = EXPERTS * CAP
PACKED = EXPERTS * GROUP
D = 2560
HALF = D // 2
HEAD = 896
TAIL = HALF - HEAD
HID = 768


def iota(shape, dim):
    return lax.broadcasted_iota(jnp.int32, shape, dim)


def picks(cond):
    return jnp.where(cond, 1.0, 0.0).astype(BF16)


def chosen_rows(pick, values):
    return jnp.dot(pick, values, preferred_element_type=F32)


def pack(head, low, high, rows):
    first = chosen_rows(head, rows[:, :HEAD])
    tail = rows[:, HEAD:]
    return (
        (first[:, :TAIL] + chosen_rows(low, tail)).astype(BF16),
        (first[:, TAIL : 2 * TAIL] + chosen_rows(high, tail)).astype(BF16),
        first[:, 2 * TAIL :].astype(BF16),
    )


def unpack(head, low, high, packed):
    first = chosen_rows(head, packed)
    tail = chosen_rows(low, packed[:, :TAIL]) + chosen_rows(high, packed[:, TAIL : 2 * TAIL])
    return first.astype(BF16), tail.astype(BF16)


def slot_maps(slot, place):
    group = (slot * 205) >> 11
    rank = slot - group * CAP
    base = slot + 6 * group
    return (
        picks(place == base),
        picks((place == base + 10) & (rank < 6)),
        picks((place == base + 4) & (rank >= 6)),
    )


def kernel(
    tok_hbm, id_ref, router_hbm, wg_hbm, wu_hbm, wd_hbm, sg_hbm, su_hbm, sd_hbm,
    out_ref,
    tok, router, wg, wu, wd, sg, su, sd,
    pos_out, pos_in, going, coming, back_going, back_coming,
    x, hid, z, y_out, y_in, r_out, r_in,
    load_sem, pos_send, pos_recv, go_send, go_recv, back_send, back_recv,
    t_send, t_recv, pair_send, pair_recv, y_send, y_recv, r_send, r_recv,
):
    s = lax.axis_index("section")
    h = lax.axis_index("expert")
    core = lax.rem(s, 2)
    sibling = s + 1 - 2 * core
    ahead = lax.rem(s + 2 * (1 - 2 * core) + SECTIONS, SECTIONS)
    behind = lax.rem(s - 2 * (1 - 2 * core) + SECTIONS, SECTIONS)
    following = lax.rem(s + 1, SECTIONS)
    previous = lax.rem(s + SECTIONS - 1, SECTIONS)

    barrier = pltpu.get_barrier_semaphore()

    def greet(j, carry):
        pl.semaphore_signal(barrier, 1, device_id={"expert": lax.rem(h + j, EXPERTS)}, device_id_type=MESH)
        return carry

    for partner in (ahead, behind, following, previous):
        pl.semaphore_signal(barrier, 1, device_id={"section": partner}, device_id_type=MESH)
    lax.fori_loop(1, EXPERTS, greet, 0)

    loads = [
        pltpu.make_async_copy(source, target, load_sem.at[number])
        for number, (source, target) in enumerate(
            [(tok_hbm, tok), (router_hbm, router), (sg_hbm, sg), (su_hbm, su), (wg_hbm, wg), (wu_hbm, wu), (sd_hbm, sd), (wd_hbm, wd)]
        )
    ]
    for load in loads:
        load.start()

    chosen = id_ref[...]
    onehot = chosen == iota((TOK, TOK), 1)
    earlier = picks(iota((TOK, TOK), 1) < iota((TOK, TOK), 0))
    before = jnp.dot(earlier, picks(onehot), preferred_element_type=F32)
    rank = jnp.sum(jnp.where(onehot, before, 0.0), axis=1, keepdims=True)
    place = chosen.astype(F32) * GROUP + rank
    pos_out[...] = jnp.broadcast_to(place, (TOK, TOK)).T[:8]

    pl.semaphore_wait(barrier, EXPERTS - 1 + 4)

    def remote(source, target, send, recv, **where):
        return pltpu.make_async_remote_copy(
            src_ref=source, dst_ref=target, send_sem=send, recv_sem=recv, device_id=where, device_id_type=MESH
        )

    pos_copy = remote(pos_out, pos_in, pos_send, pos_recv, section=previous)
    pos_copy.start()
    loads[0].wait()
    pos_copy.wait_recv()

    def group(ref, q, e):
        return ref.at[q, pl.ds(pl.multiple_of(e * GROUP, GROUP), GROUP)]

    def exchange(source, target, send, recv, q):
        def one(j, carry):
            e = lax.rem(h + j, EXPERTS)
            remote(group(source, q, e), group(target, q, h), send.at[q, e], recv.at[q, h], expert=e).start()
            return carry

        lax.fori_loop(1, EXPERTS, one, 0)
        pltpu.make_async_copy(group(source, q, h), group(target, q, h), recv.at[q, h]).start()

    def exchanged(source, target, send, recv, q):
        def one(j, carry):
            e = lax.rem(h + j, EXPERTS)
            remote(group(source, q, e), group(target, q, e), send.at[q, e], recv.at[q, e], expert=e).wait_recv()
            return carry

        lax.fori_loop(1, EXPERTS, one, 0)
        pltpu.make_async_copy(group(source, q, h), group(target, q, h), recv.at[q, h]).wait()

    def exchange_sent(source, target, send, recv, q):
        def one(j, carry):
            e = lax.rem(h + j, EXPERTS)
            remote(group(source, q, e), group(target, q, e), send.at[q, e], recv.at[q, e], expert=e).wait_send()
            return carry

        lax.fori_loop(1, EXPERTS, one, 0)

    goes = (going, coming, go_send, go_recv)
    returns = (back_going, back_coming, back_send, back_recv)

    where = pos_in[0:1, :].astype(jnp.int32)
    spot = iota((PACKED, TOK), 0)
    in_tail = (spot & (GROUP - 1)) >= CAP
    to_packed = (picks(spot == where), picks((spot == where + 10) & in_tail), picks((spot == where + 4) & in_tail))

    def put(target, q, pieces):
        target[q, :, :TAIL] = pieces[0]
        target[q, :, TAIL : 2 * TAIL] = pieces[1]
        target[q, :, 2 * TAIL :] = pieces[2]

    for q in range(2):
        put(going, q, pack(*to_packed, tok[:, q * HALF : (q + 1) * HALF]))
        exchange(*goes, q)

    own_rows, pair_rows = pl.ds(0, SLOTS), pl.ds(SLOTS, SLOTS)

    def columns(q):
        return pl.ds(q * HALF, HALF)

    def gather_step(step, q):
        source, target, device = ((0, 1, ahead), (1, 2, ahead), (0, 3, behind))[step]
        return remote(
            x.at[source, own_rows, columns(q)], x.at[target, own_rows, columns(q)],
            t_send.at[step, q], t_recv.at[step, q], section=device,
        )

    def to_pair(stage, q):
        return remote(
            x.at[stage, own_rows, columns(q)], x.at[stage, pair_rows, columns(q)],
            pair_send.at[stage, q], pair_recv.at[stage, q], section=sibling,
        )

    from_packed = slot_maps(iota((SLOTS, PACKED), 0), iota((SLOTS, PACKED), 1))
    for q in range(2):
        exchanged(*goes, q)
        first, tail = unpack(*from_packed, coming[q])
        x[0, 0:SLOTS, q * HALF : q * HALF + HEAD] = first
        x[0, 0:SLOTS, q * HALF + HEAD : (q + 1) * HALF] = tail
        gather_step(0, q).start()
        to_pair(0, q).start()
    for load in loads[1:]:
        load.wait()

    def hidden(stage):
        scores = jnp.dot(x[stage], router[...], preferred_element_type=F32)
        score = jnp.sum(jnp.where(iota(scores.shape, 1) == h, scores, 0.0), axis=1, keepdims=True)
        prob = 1.0 / (1.0 + jnp.exp(-score))
        for gate_mat, up_mat, first, scale in ((sg, su, 0, None), (wg, wu, HID, prob)):
            gate = jnp.dot(x[stage], gate_mat[...], preferred_element_type=F32)
            up = jnp.dot(x[stage], up_mat[...], preferred_element_type=F32)
            value = gate / (1.0 + jnp.exp(-gate)) * up
            if scale is not None:
                value = value * scale
            hid[:, first : first + HID] = value.astype(BF16)

    def partial_copy(stage, q):
        return remote(
            y_out.at[stage, :, columns(q)], y_in.at[stage, :, columns(q)],
            y_send.at[stage, q], y_recv.at[stage, q], section=sibling,
        )

    def down(stage):
        for q in range(2):
            cols = slice(q * HALF, (q + 1) * HALF)
            total = jnp.dot(hid[:, :HID], sd[:, cols], preferred_element_type=F32)
            total += jnp.dot(hid[:, HID:], wd[:, cols], preferred_element_type=F32)
            y_out[stage, :, cols] = total[:SLOTS].astype(BF16)
            partial_copy(stage, q).start()
            z[stage, :, cols] = total[SLOTS:]

    def settle(stage, q):
        partial_copy(stage, q).wait_recv()
        cols = slice(q * HALF, (q + 1) * HALF)
        z[stage, :, cols] += y_in[stage, :, cols].astype(F32)

    def reduce_step(step, q):
        device = (behind, ahead, ahead)[step]
        return remote(
            r_out.at[step, :, columns(q)], r_in.at[step, :, columns(q)],
            r_send.at[step, q], r_recv.at[step, q], section=device,
        )

    def send_sum(step, stage, q):
        cols = slice(q * HALF, (q + 1) * HALF)
        r_out[step, :, cols] = z[stage, :, cols].astype(BF16)
        reduce_step(step, q).start()

    def send_joined(q):
        reduce_step(1, q).wait_recv()
        cols = slice(q * HALF, (q + 1) * HALF)
        r_out[2, :, cols] = (z[core, :, cols] + r_in[1, :, cols].astype(F32)).astype(BF16)
        reduce_step(2, q).start()

    def pass_on(step, stage, forward):
        for q in range(2):
            gather_step(step, q).wait_recv()
            if forward is not None:
                gather_step(forward, q).start()
            to_pair(stage, q).start()

    def ready(stage):
        for q in range(2):
            to_pair(stage, q).wait_recv()

    ready(0)
    hidden(0)
    down(0)

    pass_on(0, 1, 1)
    for q in range(2):
        settle(0, q)
    ready(1)
    hidden(1)
    for q in range(2):
        gather_step(2, q).start()
    down(1)

    pass_on(1, 2, None)
    for q in range(2):
        settle(1, q)

    @pl.when(core == 0)
    def _():
        for q in range(2):
            send_sum(1, 1, q)

    ready(2)
    hidden(2)
    down(2)

    pass_on(2, 3, None)
    for q in range(2):
        settle(2, q)

    @pl.when(core == 1)
    def _():
        for q in range(2):
            send_sum(1, 2, q)

    ready(3)
    hidden(3)

    @pl.when(core == 0)
    def _():
        for q in range(2):
            send_joined(q)
        for q in range(2):
            send_sum(0, 2, q)

    down(3)
    for q in range(2):
        settle(3, q)

    @pl.when(core == 1)
    def _():
        for q in range(2):
            send_sum(0, 3, q)
        for q in range(2):
            send_joined(q)

    last = lax.rem(3 + core, 4)
    back_packed = slot_maps(iota((PACKED, SLOTS), 1), iota((PACKED, SLOTS), 0))
    for q in range(2):
        reduce_step(0, q).wait_recv()
        reduce_step(2, q).wait_recv()
        cols = slice(q * HALF, (q + 1) * HALF)
        final = z[last, :, cols] + r_in[0, :, cols].astype(F32) + r_in[2, :, cols].astype(F32)
        put(back_going, q, pack(*back_packed, final.astype(BF16)))
        exchange(*returns, q)

    chosen_place = place.astype(jnp.int32)
    spot = iota((TOK, PACKED), 1)
    low_rank = rank < 6.0
    home = (
        picks(spot == chosen_place),
        picks((spot == chosen_place + 10) & low_rank),
        picks((spot == chosen_place + 4) & jnp.logical_not(low_rank)),
    )
    for q in range(2):
        exchanged(*returns, q)
        first, tail = unpack(*home, back_coming[q])
        out_ref[:, q * HALF : q * HALF + HEAD] = first
        out_ref[:, q * HALF + HEAD : (q + 1) * HALF] = tail

    pos_copy.wait_send()
    for q in range(2):
        exchange_sent(*goes, q)
        exchange_sent(*returns, q)
        for step in range(3):
            gather_step(step, q).wait_send()
            reduce_step(step, q).wait_send()
        for stage in range(4):
            to_pair(stage, q).wait_send()
            partial_copy(stage, q).wait_send()


def on_device(arriving, expert_id, router, gate_weight, up_weight, down_weight, shared_gate, shared_up, shared_down):
    anywhere = pl.BlockSpec(memory_space=pl.ANY)
    vmem = pl.BlockSpec(memory_space=pltpu.VMEM)
    dma = pltpu.SemaphoreType.DMA
    rows = 8 * SLOTS
    return pl.pallas_call(
        kernel,
        out_shape=jax.ShapeDtypeStruct((TOK, D), BF16),
        in_specs=[anywhere, vmem] + [anywhere] * 7,
        out_specs=vmem,
        scratch_shapes=[
            pltpu.VMEM((TOK, D), BF16),
            pltpu.VMEM((D, EXPERTS), BF16),
            pltpu.VMEM((D, HID), BF16),
            pltpu.VMEM((D, HID), BF16),
            pltpu.VMEM((HID, D), BF16),
            pltpu.VMEM((D, HID), BF16),
            pltpu.VMEM((D, HID), BF16),
            pltpu.VMEM((HID, D), BF16),
            pltpu.VMEM((8, TOK), F32),
            pltpu.VMEM((8, TOK), F32),
            pltpu.VMEM((2, PACKED, HEAD), BF16),
            pltpu.VMEM((2, PACKED, HEAD), BF16),
            pltpu.VMEM((2, PACKED, HEAD), BF16),
            pltpu.VMEM((2, PACKED, HEAD), BF16),
            pltpu.VMEM((4, 2 * SLOTS, D), BF16),
            pltpu.VMEM((2 * SLOTS, 2 * HID), BF16),
            pltpu.VMEM((4, SLOTS, D), F32),
            pltpu.VMEM((4, SLOTS, D), BF16),
            pltpu.VMEM((4, SLOTS, D), BF16),
            pltpu.VMEM((3, SLOTS, D), BF16),
            pltpu.VMEM((3, SLOTS, D), BF16),
            dma((8,)),
            dma,
            dma,
            dma((2, EXPERTS)),
            dma((2, EXPERTS)),
            dma((2, EXPERTS)),
            dma((2, EXPERTS)),
            dma((3, 2)),
            dma((3, 2)),
            dma((4, 2)),
            dma((4, 2)),
            dma((4, 2)),
            dma((4, 2)),
            dma((3, 2)),
            dma((3, 2)),
        ],
        compiler_params=pltpu.CompilerParams(
            collective_id=0, has_side_effects=True, vmem_limit_bytes=62 * 2**20
        ),
        cost_estimate=pl.CostEstimate(
            flops=2 * rows * D * HID * 6, bytes_accessed=12 * D * HID + 4 * TOK * D, transcendentals=2 * rows * HID
        ),
    )(
        arriving, expert_id, router, gate_weight[0], up_weight[0], down_weight[0], shared_gate, shared_up, shared_down
    )


def solution(mesh):
    placed = (
        P(("section", "expert"), None),
        P(("section", "expert"), None),
        P(),
        P("expert", None, "section"),
        P("expert", None, "section"),
        P("expert", "section", None),
        P(None, "section"),
        P(None, "section"),
        P("section", None),
    )
    return jax.shard_map(
        on_device,
        mesh=mesh,
        in_specs=placed,
        out_specs=P(("section", "expert"), None),
        check_vma=False,
    )
```

time: 336 us -> 106 us (0.32); the launches traced: 330 us -> 106 us
  waiting for transfers between devices: 191 us -> 0 us
  Pallas kernels: 0 us -> 101 us
  matrix products: 60.6 us -> 0 us
  blocking collectives: 24 us -> 0 us
  other arithmetic: 21.1 us -> 0 us
  between operations: 13.2 us -> 0.01 us
  starting transfers between devices: 9.61 us -> 0 us
  local copies, waits for them, and re-layouts: 10.5 us -> 5.31 us
    reduce_scatter x1 -> x0, waiting for transfers between devices: 123 us -> none  [on_device(): lax.psum_scatter(joined.reshape(lax.axis_size('section') * group_rows, mo...]
    pallas_call x0 -> x1, Pallas kernels: none -> 101 us  [on_device(): pl.pallas_call(kernel, out_shape=jax.ShapeDtypeStruct((TOK, D), BF16), in...]
    dot_general x5 -> x0, matrix products: 60.6 us -> none  [the longest x1 21.3 us: on_device(): jnp.dot(routed_hidden, down_local, preferred_element_type=jnp.float32)]
    all_to_all x1 -> x0, waiting for transfers between devices: 32.2 us -> none  [on_device(): lax.all_to_all(summed[:slot_count].reshape(experts, capacity, model_width...]
    all_gather x2 -> x0, waiting for transfers between devices: 28 us -> none  [the longest x1 18.5 us: on_device(): lax.all_gather(slot_rows_here, 'section', axis=0, tiled=True)]
    all_to_all x1 -> x0, blocking collectives: 24 us -> none  [on_device(): lax.all_to_all(outgoing.reshape(experts, capacity, model_width), 'expert'...]
    concatenate x1 -> x0, other arithmetic: 16.3 us -> none  [on_device(): jnp.concatenate([routed.reshape(groups, slot_count, model_width), shared....]
    ppermute x1 -> x0, waiting for transfers between devices: 7.85 us -> none  [passed_along(): return lax.ppermute(value, axis, pairs)]
  transfers between devices with their start and end apart: 5 -> 0, of which waited for: 5 -> 0; matrix products, arithmetic and copies ran while one was open for 9% -> 0% of each run, Pallas kernels for 0% -> 0%
where the time goes in v1:
time: 106 us
  Pallas kernels  101 us (95%)
  local copies, waits for them, and re-layouts  5.31 us (5%)
    pallas_call x1, Pallas kernels, on_device(): pl.pallas_call(kernel, out_shape=jax.ShapeDtypeStruct((TOK, D), BF16), in...  101 us
    unnamed x3, local copies, waits for them, and re-layouts  5.31 us

profile of v1, /device:TPU:1, one launch (start us, length us, event | category | flops | bytes accessed | tf_op | source)
XLA Modules:
  0.0 106.0 jit_solution(3294858811805805447)
XLA Ops:
  0.0 1.4 %copy.10.id_ref = s32[128,1]{1,0:T(8,128)} copy(s32[128,1]{0,1:T(1,128)} %param.10) | data formatting | bytes 1024 | tf_op args[1]
  1.4 2.0 %copy.11.router_hbm = bf16[2560,16]{1,0:T(8,128)(2,1)} copy(bf16[2560,16]{0,1:T(8,128)(2,1)} %param.11) | data formatting | bytes 163840 | tf_op args[2]
  3.3 100.7 %shard_map.91 = bf16[128,2560]{1,0:T(8,128)(2,1)} custom-call(bf16[128,2560]{1,0:T(8,128)(2,1)} %tok_hbm.1, s32[128,1]{1,0:T(8,128)} %copy.10.id_ref, bf16[2560,16]{1,0:T(8,128)(2,1)} %copy.11.router_hbm, bf16[2560,768]{1,0:T(8,128)(2,1)} %bitcast.3, bf16[2560,768]{1,0:T(8,128)(2,1)} %bitcast.4, bf16[768,2560]{1,0:T(8,128)(2,1)} %bitcast.5, ...), custom_call_target="tpu_custom_call" | custom-call | flops 30198988800 | bytes 24903680 | tf_op jit(solution)/shard_map/pallas_call | solution.py:355
  104.0 2.0 %copy.13 = bf16[128,2560]{1,0:T(8,128)(2,1)} copy(bf16[128,2560]{1,0:T(8,128)(2,1)} %shard_map.91) | data formatting | bytes 1310720

commit v2 on v1

v2 whole, which is shorter than its diff:
```python
import jax
import jax.numpy as jnp
from jax import lax
from jax.experimental import pallas as pl
from jax.experimental.pallas import tpu as pltpu
from jax.sharding import PartitionSpec as P

MESH = pl.DeviceIdType.MESH
F32 = jnp.float32
BF16 = jnp.bfloat16

SECTIONS = 8
EXPERTS = 16
TOK = 128
CAP = 10
GROUP = 16
SLOTS = EXPERTS * CAP
PACKED = EXPERTS * GROUP
D = 2560
PARTS = 5
WIDE = D // PARTS
HEAD = 384
TAIL = WIDE - HEAD
HID = 768


def iota(shape, dim):
    return lax.broadcasted_iota(jnp.int32, shape, dim)


def picks(cond):
    return jnp.where(cond, 1.0, 0.0).astype(BF16)


def chosen_rows(pick, values):
    return jnp.dot(pick, values, preferred_element_type=F32)


def pack(head, low, high, rows):
    first = chosen_rows(head, rows[:, :HEAD])
    tail = rows[:, HEAD:]
    return (
        (first[:, :TAIL] + chosen_rows(low, tail)).astype(BF16),
        (first[:, TAIL : 2 * TAIL] + chosen_rows(high, tail)).astype(BF16),
        first[:, 2 * TAIL :].astype(BF16),
    )


def unpack(head, low, high, packed):
    first = chosen_rows(head, packed)
    tail = chosen_rows(low, packed[:, :TAIL]) + chosen_rows(high, packed[:, TAIL : 2 * TAIL])
    return first.astype(BF16), tail.astype(BF16)


def slot_maps(slot, place):
    group = (slot * 205) >> 11
    rank = slot - group * CAP
    base = slot + 6 * group
    return (
        picks(place == base),
        picks((place == base + 10) & (rank < 6)),
        picks((place == base + 4) & (rank >= 6)),
    )


def kernel(
    tok_hbm, id_ref, router_hbm, wg_hbm, wu_hbm, wd_hbm, sg_hbm, su_hbm, sd_hbm,
    out_ref,
    tok, router, wg, wu, sg, su, both_down,
    pos_out, pos_in, going, coming, back_coming,
    x, hid, z, y_out, y_in, r_out, r_in,
    load_sem, pos_send, pos_recv, go_send, go_recv, back_send, back_recv,
    t_send, t_recv, pair_send, pair_recv, y_send, y_recv, r_send, r_recv,
):
    s = lax.axis_index("section")
    h = lax.axis_index("expert")
    core = lax.rem(s, 2)
    sibling = s + 1 - 2 * core
    ahead = lax.rem(s + 2 * (1 - 2 * core) + SECTIONS, SECTIONS)
    behind = lax.rem(s - 2 * (1 - 2 * core) + SECTIONS, SECTIONS)
    following = lax.rem(s + 1, SECTIONS)
    previous = lax.rem(s + SECTIONS - 1, SECTIONS)

    barrier = pltpu.get_barrier_semaphore()

    def greet(j, carry):
        pl.semaphore_signal(barrier, 1, device_id={"expert": lax.rem(h + j, EXPERTS)}, device_id_type=MESH)
        return carry

    for partner in (ahead, behind, following, previous):
        pl.semaphore_signal(barrier, 1, device_id={"section": partner}, device_id_type=MESH)
    lax.fori_loop(1, EXPERTS, greet, 0)

    loads = [
        pltpu.make_async_copy(source, target, load_sem.at[number])
        for number, (source, target) in enumerate(
            [(tok_hbm, tok), (router_hbm, router), (sg_hbm, sg), (su_hbm, su), (wg_hbm, wg), (wu_hbm, wu), (sd_hbm, both_down.at[pl.ds(0, HID)]), (wd_hbm, both_down.at[pl.ds(HID, HID)])]
        )
    ]
    for load in loads:
        load.start()

    chosen = id_ref[...]
    onehot = iota((EXPERTS, TOK), 0) == chosen
    earlier = picks(iota((TOK, TOK), 0) < iota((TOK, TOK), 1))
    before = jnp.dot(picks(onehot), earlier, preferred_element_type=F32)
    rank = jnp.sum(jnp.where(onehot, before, 0.0), axis=0, keepdims=True)
    place = chosen.astype(F32) * GROUP + rank
    pos_out[...] = jnp.broadcast_to(place, (8, TOK))

    pl.semaphore_wait(barrier, EXPERTS - 1 + 4)

    def remote(source, target, send, recv, **where):
        return pltpu.make_async_remote_copy(
            src_ref=source, dst_ref=target, send_sem=send, recv_sem=recv, device_id=where, device_id_type=MESH
        )

    pos_copy = remote(pos_out, pos_in, pos_send, pos_recv, section=previous)
    pos_copy.start()
    loads[0].wait()
    pos_copy.wait_recv()

    def group(ref, q, e):
        return ref.at[q, pl.ds(pl.multiple_of(e * GROUP, GROUP), GROUP)]

    def exchange(source, target, send, recv, q):
        def one(j, carry):
            e = lax.rem(h + j, EXPERTS)
            remote(group(source, q, e), group(target, q, h), send.at[q, e], recv.at[q, h], expert=e).start()
            return carry

        lax.fori_loop(1, EXPERTS, one, 0)
        pltpu.make_async_copy(group(source, q, h), group(target, q, h), recv.at[q, h]).start()

    def exchanged(source, target, send, recv, q):
        def one(j, carry):
            e = lax.rem(h + j, EXPERTS)
            remote(group(source, q, e), group(target, q, e), send.at[q, e], recv.at[q, e], expert=e).wait_recv()
            return carry

        lax.fori_loop(1, EXPERTS, one, 0)
        pltpu.make_async_copy(group(source, q, h), group(target, q, h), recv.at[q, h]).wait()

    def exchange_sent(source, target, send, recv, q):
        def one(j, carry):
            e = lax.rem(h + j, EXPERTS)
            remote(group(source, q, e), group(target, q, e), send.at[q, e], recv.at[q, e], expert=e).wait_send()
            return carry

        lax.fori_loop(1, EXPERTS, one, 0)

    goes = (going, coming, go_send, go_recv)
    returns = (going, back_coming, back_send, back_recv)

    where = pos_in[0:1, :].astype(jnp.int32)
    spot = iota((PACKED, TOK), 0)
    in_tail = (spot & (GROUP - 1)) >= CAP
    to_packed = (picks(spot == where), picks((spot == where + 10) & in_tail), picks((spot == where + 4) & in_tail))

    def put(target, q, pieces):
        target[q, :, :TAIL] = pieces[0]
        target[q, :, TAIL : 2 * TAIL] = pieces[1]
        target[q, :, 2 * TAIL :] = pieces[2]

    for q in range(PARTS):
        put(going, q, pack(*to_packed, tok[:, q * WIDE : (q + 1) * WIDE]))
        exchange(*goes, q)

    own_rows, pair_rows = pl.ds(0, SLOTS), pl.ds(SLOTS, SLOTS)

    def columns(q):
        return pl.ds(q * WIDE, WIDE)

    def gather_step(step, q):
        source, target, device = ((0, 1, ahead), (1, 2, ahead), (0, 3, behind))[step]
        return remote(
            x.at[source, own_rows, columns(q)], x.at[target, own_rows, columns(q)],
            t_send.at[step, q], t_recv.at[step, q], section=device,
        )

    def to_pair(stage, q):
        return remote(
            x.at[stage, own_rows, columns(q)], x.at[stage, pair_rows, columns(q)],
            pair_send.at[stage, q], pair_recv.at[stage, q], section=sibling,
        )

    def pass_on(step, q):
        gather_step(step, q).wait_recv()
        to_pair(step + 1, q).start()

    def ready(stage):
        for q in range(PARTS):
            to_pair(stage, q).wait_recv()

    def activate(first, gate, up, scale):
        value = gate / (1.0 + jnp.exp(-gate)) * up
        if scale is not None:
            value = value * scale
        hid[:, first : first + HID] = value.astype(BF16)

    def probs(stage):
        scores = lax.dot_general(x[stage], router[...], (((1,), (1,)), ((), ())), preferred_element_type=F32)
        score = jnp.sum(jnp.where(iota(scores.shape, 1) == h, scores, 0.0), axis=1, keepdims=True)
        return 1.0 / (1.0 + jnp.exp(-score))

    mats = (sg, su, wg, wu)

    def kept(number, part):
        place_of = 2 * number + part
        first = place_of % 3 * HID
        return 1 + place_of // 3, slice(first, first + HID)

    def added(number, q):
        cols = slice(q * WIDE, (q + 1) * WIDE)
        total = jnp.dot(x[0, :, cols], mats[number][cols, :], preferred_element_type=F32)
        if q == 0:
            return total
        halves = [z[kept(number, part)[0], :, kept(number, part)[1]] for part in range(2)]
        return total + jnp.concatenate(halves, axis=0)

    def widen(q):
        to_pair(0, q).wait_recv()
        for number in range(4):
            total = added(number, q)
            for part in range(2):
                level, cols = kept(number, part)
                z[level, :, cols] = total[part * SLOTS : (part + 1) * SLOTS]

    def partial_copy(stage, q):
        return remote(
            y_out.at[stage, :, columns(q)], y_in.at[stage, :, columns(q)],
            y_send.at[stage, q], y_recv.at[stage, q], section=sibling,
        )

    def down(stage, after):
        for q in range(PARTS):
            cols = slice(q * WIDE, (q + 1) * WIDE)
            total = jnp.dot(hid[...], both_down[:, cols], preferred_element_type=F32)
            y_out[stage, :, cols] = total[:SLOTS].astype(BF16)
            partial_copy(stage, q).start()
            z[stage, :, cols] = total[SLOTS:]
            after(q)

    def chip_sum(stage, q):
        partial_copy(stage, q).wait_recv()
        cols = slice(q * WIDE, (q + 1) * WIDE)
        return z[stage, :, cols] + y_in[stage, :, cols].astype(F32)

    def reduce_step(step, q):
        return remote(
            r_out.at[step, :, columns(q)], r_in.at[step, :, columns(q)],
            r_send.at[step, q], r_recv.at[step, q], section=(ahead, behind, behind)[step],
        )

    def send_sum(step, stage, q):
        r_out[step, :, q * WIDE : (q + 1) * WIDE] = chip_sum(stage, q).astype(BF16)
        reduce_step(step, q).start()

    def send_joined(stage, q):
        reduce_step(1, q).wait_recv()
        cols = slice(q * WIDE, (q + 1) * WIDE)
        r_out[2, :, cols] = (chip_sum(stage, q) + r_in[1, :, cols].astype(F32)).astype(BF16)
        reduce_step(2, q).start()

    def nothing(*_):
        pass

    def on_core(which, action, *steps):
        @pl.when(core == which)
        def _():
            for step in steps:
                action(*step)

    def hidden(stage, between):
        ready(stage)
        gate = jnp.dot(x[stage], sg[...], preferred_element_type=F32)
        up = jnp.dot(x[stage], su[...], preferred_element_type=F32)
        activate(0, gate, up, None)
        between()
        gate = jnp.dot(x[stage], wg[...], preferred_element_type=F32)
        up = jnp.dot(x[stage], wu[...], preferred_element_type=F32)
        activate(HID, gate, up, probs(stage))

    from_packed = slot_maps(iota((SLOTS, PACKED), 0), iota((SLOTS, PACKED), 1))
    for q in range(PARTS):
        exchanged(*goes, q)
        first, tail = unpack(*from_packed, coming[q])
        x[0, 0:SLOTS, q * WIDE : q * WIDE + HEAD] = first
        x[0, 0:SLOTS, q * WIDE + HEAD : (q + 1) * WIDE] = tail
        gather_step(0, q).start()
        to_pair(0, q).start()
        if q == 0:
            for load in loads[1:]:
                load.wait()
        if q >= 1:
            widen(q - 1)
        if q >= 2:
            pass_on(0, q - 2)
        if q >= 3:
            gather_step(1, q - 3).start()

    every = range(PARTS)
    last_part = PARTS - 1
    to_pair(0, last_part).wait_recv()
    activate(0, added(0, last_part), added(1, last_part), None)
    pass_on(0, last_part - 1)
    gather_step(1, last_part - 2).start()
    activate(HID, added(2, last_part), added(3, last_part), probs(0))
    pass_on(0, last_part)
    gather_step(1, last_part - 1).start()
    gather_step(1, last_part).start()
    down(0, nothing)

    for q in every:
        gather_step(2, q).start()
    hidden(1, nothing)
    for q in every:
        pass_on(1, q)
    down(1, lambda q: on_core(0, send_sum, (1, 1, q - 2)) if q >= 2 else None)

    on_core(0, send_sum, *[(0, 0, q) for q in every])
    hidden(2, lambda: on_core(0, send_sum, (1, 1, PARTS - 2), (1, 1, PARTS - 1)))
    for q in every:
        pass_on(2, q)
    down(2, lambda q: on_core(1, send_sum, (1, 2, q - 2)) if q >= 2 else None)

    on_core(1, send_sum, *[(0, 1, q) for q in every])

    def between():
        on_core(1, send_sum, (1, 2, PARTS - 2), (1, 2, PARTS - 1))
        on_core(0, send_joined, *[(2, q) for q in every])

    hidden(3, between)
    for q in every:
        exchange_sent(*goes, q)
    down(3, lambda q: on_core(1, send_joined, (3, q - 2)) if q >= 2 else None)
    on_core(1, send_joined, (3, PARTS - 2), (3, PARTS - 1))

    last = lax.rem(3 + core, 4)
    back_packed = slot_maps(iota((PACKED, SLOTS), 1), iota((PACKED, SLOTS), 0))
    chosen_place = jnp.broadcast_to(place, (TOK, TOK)).T[:, 0:1].astype(jnp.int32)
    spot = iota((TOK, PACKED), 1)
    low_rank = (chosen_place & (GROUP - 1)) < 6
    home = (
        picks(spot == chosen_place),
        picks((spot == chosen_place + 10) & low_rank),
        picks((spot == chosen_place + 4) & jnp.logical_not(low_rank)),
    )
    for q in range(PARTS):
        reduce_step(0, q).wait_recv()
        reduce_step(2, q).wait_recv()
        partial_copy(last, q).wait_recv()
        cols = slice(q * WIDE, (q + 1) * WIDE)
        final = z[last, :, cols] + y_in[last, :, cols].astype(F32)
        final += r_in[0, :, cols].astype(F32) + r_in[2, :, cols].astype(F32)
        put(going, q, pack(*back_packed, final.astype(BF16)))
        exchange(*returns, q)

    for q in range(PARTS):
        exchanged(*returns, q)
        first, tail = unpack(*home, back_coming[q])
        out_ref[:, q * WIDE : q * WIDE + HEAD] = first
        out_ref[:, q * WIDE + HEAD : (q + 1) * WIDE] = tail

    pos_copy.wait_send()
    for q in range(PARTS):
        exchange_sent(*returns, q)
        for step in range(3):
            gather_step(step, q).wait_send()
            reduce_step(step, q).wait_send()
        for stage in range(4):
            to_pair(stage, q).wait_send()
            partial_copy(stage, q).wait_send()


def on_device(arriving, expert_id, router, gate_weight, up_weight, down_weight, shared_gate, shared_up, shared_down):
    anywhere = pl.BlockSpec(memory_space=pl.ANY)
    vmem = pl.BlockSpec(memory_space=pltpu.VMEM)
    dma = pltpu.SemaphoreType.DMA
    rows = 8 * SLOTS
    return pl.pallas_call(
        kernel,
        out_shape=jax.ShapeDtypeStruct((TOK, D), BF16),
        in_specs=[anywhere, vmem] + [anywhere] * 7,
        out_specs=vmem,
        scratch_shapes=[
            pltpu.VMEM((TOK, D), BF16),
            pltpu.VMEM((EXPERTS, D), BF16),
            pltpu.VMEM((D, HID), BF16),
            pltpu.VMEM((D, HID), BF16),
            pltpu.VMEM((D, HID), BF16),
            pltpu.VMEM((D, HID), BF16),
            pltpu.VMEM((2 * HID, D), BF16),
            pltpu.VMEM((8, TOK), F32),
            pltpu.VMEM((8, TOK), F32),
            pltpu.VMEM((PARTS, PACKED, HEAD), BF16),
            pltpu.VMEM((PARTS, PACKED, HEAD), BF16),
            pltpu.VMEM((PARTS, PACKED, HEAD), BF16),
            pltpu.VMEM((4, 2 * SLOTS, D), BF16),
            pltpu.VMEM((2 * SLOTS, 2 * HID), BF16),
            pltpu.VMEM((4, SLOTS, D), F32),
            pltpu.VMEM((4, SLOTS, D), BF16),
            pltpu.VMEM((4, SLOTS, D), BF16),
            pltpu.VMEM((3, SLOTS, D), BF16),
            pltpu.VMEM((3, SLOTS, D), BF16),
            dma((8,)),
            dma,
            dma,
            dma((PARTS, EXPERTS)),
            dma((PARTS, EXPERTS)),
            dma((PARTS, EXPERTS)),
            dma((PARTS, EXPERTS)),
            dma((3, PARTS)),
            dma((3, PARTS)),
            dma((4, PARTS)),
            dma((4, PARTS)),
            dma((4, PARTS)),
            dma((4, PARTS)),
            dma((3, PARTS)),
            dma((3, PARTS)),
        ],
        compiler_params=pltpu.CompilerParams(
            collective_id=0, has_side_effects=True, vmem_limit_bytes=62 * 2**20
        ),
        cost_estimate=pl.CostEstimate(
            flops=2 * rows * D * HID * 6, bytes_accessed=12 * D * HID + 4 * TOK * D, transcendentals=2 * rows * HID
        ),
    )(
        arriving, expert_id.reshape(1, TOK), router.T, gate_weight[0], up_weight[0], down_weight[0], shared_gate, shared_up, shared_down
    )


def solution(mesh):
    placed = (
        P(("section", "expert"), None),
        P(("section", "expert"), None),
        P(),
        P("expert", None, "section"),
        P("expert", None, "section"),
        P("expert", "section", None),
        P(None, "section"),
        P(None, "section"),
        P("section", None),
    )
    return jax.shard_map(
        on_device,
        mesh=mesh,
        in_specs=placed,
        out_specs=P(("section", "expert"), None),
        check_vma=False,
    )
```

time: 106 us -> 90.4 us (0.85)
  Pallas kernels: 101 us -> 88.3 us
  local copies, waits for them, and re-layouts: 5.31 us -> 1.97 us
    pallas_call x1, Pallas kernels: 101 us -> 88.3 us  [on_device(): pl.pallas_call(kernel, out_shape=jax.ShapeDtypeStruct((TOK, D), BF16), in...]
    unnamed x3 -> x1, local copies, waits for them, and re-layouts: 5.31 us -> 1.97 us
where the time goes in v2:
time: 90.4 us; the launch traced here: 90.2 us
  Pallas kernels  88.3 us (98%)
  local copies, waits for them, and re-layouts  1.97 us (2%)
    pallas_call x1, Pallas kernels, on_device(): pl.pallas_call(kernel, out_shape=jax.ShapeDtypeStruct((TOK, D), BF16), in...  88.3 us
    unnamed x1, local copies, waits for them, and re-layouts  1.97 us

profile of v2, /device:TPU:1, one launch (start us, length us, event | category | flops | bytes accessed | tf_op | source)
XLA Modules:
  0.0 90.2 jit_solution(4274037501479469694)
XLA Ops:
  0.0 88.3 %shard_map.91 = bf16[128,2560]{1,0:T(8,128)(2,1)} custom-call(bf16[128,2560]{1,0:T(8,128)(2,1)} %tok_hbm.1, s32[1,128]{1,0:T(1,128)} %bitcast.9, bf16[16,2560]{1,0:T(8,128)(2,1)} %bitcast.8, bf16[2560,768]{1,0:T(8,128)(2,1)} %bitcast.5, bf16[2560,768]{1,0:T(8,128)(2,1)} %bitcast.6, bf16[768,2560]{1,0:T(8,128)(2,1)} %bitcast.7, bf16[2560,768]{1,0:T(8,128)(2,1)} %sg_hbm.1, ...), custom_call_target="tpu_custom_call" | custom-call | flops 30198988800 | bytes 24903680 | tf_op jit(solution)/shard_map/pallas_call | solution.py:381
  88.3 2.0 %copy.11 = bf16[128,2560]{1,0:T(8,128)(2,1)} copy(bf16[128,2560]{1,0:T(8,128)(2,1)} %shard_map.91) | data formatting | bytes 1310720

commit v3 on v2

--- a/solution.py
+++ b/solution.py
@@ -68,9 +68,9 @@
     out_ref,
     tok, router, wg, wu, sg, su, both_down,
     pos_out, pos_in, going, coming, back_coming,
-    x, hid, z, y_out, y_in, r_out, r_in,
+    x, probs, hid, z, y_out, y_in, r_out, r_in,
     load_sem, pos_send, pos_recv, go_send, go_recv, back_send, back_recv,
-    t_send, t_recv, pair_send, pair_recv, y_send, y_recv, r_send, r_recv,
+    t_send, t_recv, pair_send, pair_recv, prob_send, prob_recv, y_send, y_recv, r_send, r_recv,
 ):
     s = lax.axis_index("section")
     h = lax.axis_index("expert")
@@ -171,37 +171,59 @@
     def columns(q):
         return pl.ds(q * WIDE, WIDE)
 
-    def gather_step(step, q):
-        source, target, device = ((0, 1, ahead), (1, 2, ahead), (0, 3, behind))[step]
+    def span(q):
+        return pl.ds(0, D) if q is None else columns(q)
+
+    hops = ((0, 1, ahead), (1, 2, ahead), (0, 3, behind))
+
+    def gather_step(step, q=None):
+        source, target, device = hops[step]
         return remote(
-            x.at[source, own_rows, columns(q)], x.at[target, own_rows, columns(q)],
-            t_send.at[step, q], t_recv.at[step, q], section=device,
-        )
-
-    def to_pair(stage, q):
+            x.at[source, own_rows, span(q)], x.at[target, own_rows, span(q)],
+            t_send.at[step, q or 0], t_recv.at[step, q or 0], section=device,
+        )
+
+    def to_pair(stage, q=None):
         return remote(
-            x.at[stage, own_rows, columns(q)], x.at[stage, pair_rows, columns(q)],
-            pair_send.at[stage, q], pair_recv.at[stage, q], section=sibling,
-        )
-
-    def pass_on(step, q):
-        gather_step(step, q).wait_recv()
-        to_pair(step + 1, q).start()
+            x.at[stage, own_rows, span(q)], x.at[stage, pair_rows, span(q)],
+            pair_send.at[stage, q or 0], pair_recv.at[stage, q or 0], section=sibling,
+        )
+
+    def gather_probs(step):
+        source, target, device = hops[step]
+        return remote(probs.at[source, 0], probs.at[target, 0], prob_send.at[step], prob_recv.at[step], section=device)
+
+    def probs_to_pair(stage):
+        return remote(probs.at[stage, 0], probs.at[stage, 1], prob_send.at[3 + stage], prob_recv.at[3 + stage], section=sibling)
+
+    def pass_on(step, parts):
+        for q in parts:
+            gather_step(step, q).wait_recv()
+        for q in parts:
+            to_pair(step + 1, q).start()
+
+    def pass_probs(step):
+        gather_probs(step).wait_recv()
+        if step == 0:
+            gather_probs(1).start()
+        probs_to_pair(step + 1).start()
 
     def ready(stage):
         for q in range(PARTS):
             to_pair(stage, q).wait_recv()
 
-    def activate(first, gate, up, scale):
+    def activate(first, gate, up, scales=None):
         value = gate / (1.0 + jnp.exp(-gate)) * up
-        if scale is not None:
-            value = value * scale
-        hid[:, first : first + HID] = value.astype(BF16)
-
-    def probs(stage):
-        scores = lax.dot_general(x[stage], router[...], (((1,), (1,)), ((), ())), preferred_element_type=F32)
-        score = jnp.sum(jnp.where(iota(scores.shape, 1) == h, scores, 0.0), axis=1, keepdims=True)
-        return 1.0 / (1.0 + jnp.exp(-score))
+        if scales is not None:
+            for part, scale in enumerate(scales):
+                rows = slice(part * SLOTS, (part + 1) * SLOTS)
+                hid[rows, first : first + HID] = (value[rows] * scale).astype(BF16)
+        else:
+            hid[:, first : first + HID] = value.astype(BF16)
+
+    def scales(stage):
+        probs_to_pair(stage).wait_recv()
+        return [jnp.broadcast_to(probs[stage, part, 0:1, :], (TOK, 2 * TOK)).T[:SLOTS, 0:1] for part in range(2)]
 
     mats = (sg, su, wg, wu)
 
@@ -248,8 +270,8 @@
 
     def reduce_step(step, q):
         return remote(
-            r_out.at[step, :, columns(q)], r_in.at[step, :, columns(q)],
-            r_send.at[step, q], r_recv.at[step, q], section=(ahead, behind, behind)[step],
+            r_out.at[step, :, span(q)], r_in.at[step, :, span(q)],
+            r_send.at[step, q or 0], r_recv.at[step, q or 0], section=(ahead, behind, behind)[step],
         )
 
     def send_sum(step, stage, q):
@@ -275,13 +297,15 @@
         ready(stage)
         gate = jnp.dot(x[stage], sg[...], preferred_element_type=F32)
         up = jnp.dot(x[stage], su[...], preferred_element_type=F32)
-        activate(0, gate, up, None)
+        activate(0, gate, up)
         between()
         gate = jnp.dot(x[stage], wg[...], preferred_element_type=F32)
         up = jnp.dot(x[stage], wu[...], preferred_element_type=F32)
-        activate(HID, gate, up, probs(stage))
+        activate(HID, gate, up, scales(stage))
 
     from_packed = slot_maps(iota((SLOTS, PACKED), 0), iota((SLOTS, PACKED), 1))
+    probs[0, 0] = jnp.zeros((8, 2 * TOK), F32)
+    scores = jnp.zeros((EXPERTS, SLOTS), F32)
     for q in range(PARTS):
         exchanged(*goes, q)
         first, tail = unpack(*from_packed, coming[q])
@@ -294,34 +318,45 @@
                 load.wait()
         if q >= 1:
             widen(q - 1)
+        scores += lax.dot_general(
+            router[:, q * WIDE : (q + 1) * WIDE], x[0, 0:SLOTS, q * WIDE : (q + 1) * WIDE],
+            (((1,), (1,)), ((), ())), preferred_element_type=F32,
+        )
         if q >= 2:
-            pass_on(0, q - 2)
+            pass_on(0, (q - 2,))
         if q >= 3:
             gather_step(1, q - 3).start()
+
+    score = jnp.sum(jnp.where(iota(scores.shape, 0) == h, scores, 0.0), axis=0, keepdims=True)
+    probs[0, 0, :, :SLOTS] = jnp.broadcast_to(1.0 / (1.0 + jnp.exp(-score)), (8, SLOTS))
+    gather_probs(0).start()
+    gather_probs(2).start()
+    probs_to_pair(0).start()
 
     every = range(PARTS)
     last_part = PARTS - 1
     to_pair(0, last_part).wait_recv()
-    activate(0, added(0, last_part), added(1, last_part), None)
-    pass_on(0, last_part - 1)
+    activate(0, added(0, last_part), added(1, last_part))
+    pass_on(0, (last_part - 1,))
     gather_step(1, last_part - 2).start()
-    activate(HID, added(2, last_part), added(3, last_part), probs(0))
-    pass_on(0, last_part)
+    activate(HID, added(2, last_part), added(3, last_part), scales(0))
+    pass_on(0, (last_part,))
     gather_step(1, last_part - 1).start()
     gather_step(1, last_part).start()
+    pass_probs(0)
     down(0, nothing)
 
     for q in every:
         gather_step(2, q).start()
     hidden(1, nothing)
-    for q in every:
-        pass_on(1, q)
+    pass_on(1, every)
+    pass_probs(1)
     down(1, lambda q: on_core(0, send_sum, (1, 1, q - 2)) if q >= 2 else None)
 
-    on_core(0, send_sum, *[(0, 0, q) for q in every])
-    hidden(2, lambda: on_core(0, send_sum, (1, 1, PARTS - 2), (1, 1, PARTS - 1)))
-    for q in every:
-        pass_on(2, q)
+    on_core(0, send_sum, (1, 1, PARTS - 2), (1, 1, PARTS - 1))
+    hidden(2, lambda: on_core(0, send_sum, *[(0, 0, q) for q in every]))
+    pass_on(2, every)
+    pass_probs(2)
     down(2, lambda q: on_core(1, send_sum, (1, 2, q - 2)) if q >= 2 else None)
 
     on_core(1, send_sum, *[(0, 1, q) for q in every])
@@ -363,14 +398,20 @@
         out_ref[:, q * WIDE + HEAD : (q + 1) * WIDE] = tail
 
     pos_copy.wait_send()
+    for step in range(3):
+        gather_probs(step).wait_send()
+    for stage in range(4):
+        probs_to_pair(stage).wait_send()
     for q in range(PARTS):
         exchange_sent(*returns, q)
-        for step in range(3):
+        for step in range(2):
             gather_step(step, q).wait_send()
-            reduce_step(step, q).wait_send()
+            reduce_step(step + 1, q).wait_send()
+        reduce_step(0, q).wait_send()
+        gather_step(2, q).wait_send()
         for stage in range(4):
+            partial_copy(stage, q).wait_send()
             to_pair(stage, q).wait_send()
-            partial_copy(stage, q).wait_send()
 
 
 def on_device(arriving, expert_id, router, gate_weight, up_weight, down_weight, shared_gate, shared_up, shared_down):
@@ -397,6 +438,7 @@
             pltpu.VMEM((PARTS, PACKED, HEAD), BF16),
             pltpu.VMEM((PARTS, PACKED, HEAD), BF16),
             pltpu.VMEM((4, 2 * SLOTS, D), BF16),
+            pltpu.VMEM((4, 2, 8, 2 * TOK), F32),
             pltpu.VMEM((2 * SLOTS, 2 * HID), BF16),
             pltpu.VMEM((4, SLOTS, D), F32),
             pltpu.VMEM((4, SLOTS, D), BF16),
@@ -414,6 +456,8 @@
             dma((3, PARTS)),
             dma((4, PARTS)),
             dma((4, PARTS)),
+            dma((7,)),
+            dma((7,)),
             dma((4, PARTS)),
             dma((4, PARTS)),
             dma((3, PARTS)),

time: 90.4 us -> 92.8 us (1.027)
  Pallas kernels: 88.3 us -> 90.7 us
    pallas_call x1, Pallas kernels: 88.3 us -> 90.7 us  [on_device(): pl.pallas_call(kernel, out_shape=jax.ShapeDtypeStruct((TOK, D), BF16), in...]
where the time goes in v3:
time: 92.8 us; the launch traced here: 92.7 us
  Pallas kernels  90.7 us (98%)
  local copies, waits for them, and re-layouts  1.97 us (2%)
    pallas_call x1, Pallas kernels, on_device(): pl.pallas_call(kernel, out_shape=jax.ShapeDtypeStruct((TOK, D), BF16), in...  90.7 us
    unnamed x1, local copies, waits for them, and re-layouts  1.97 us

profile of v3, /device:TPU:1, one launch (start us, length us, event | category | flops | bytes accessed | tf_op | source)
XLA Modules:
  0.0 92.7 jit_solution(3742236332704944673)
XLA Ops:
  0.0 90.7 %shard_map.91 = bf16[128,2560]{1,0:T(8,128)(2,1)} custom-call(bf16[128,2560]{1,0:T(8,128)(2,1)} %tok_hbm.1, s32[1,128]{1,0:T(1,128)} %bitcast.9, bf16[16,2560]{1,0:T(8,128)(2,1)} %bitcast.8, bf16[2560,768]{1,0:T(8,128)(2,1)} %bitcast.5, bf16[2560,768]{1,0:T(8,128)(2,1)} %bitcast.6, bf16[768,2560]{1,0:T(8,128)(2,1)} %bitcast.7, bf16[2560,768]{1,0:T(8,128)(2,1)} %sg_hbm.1, ...), custom_call_target="tpu_custom_call" | custom-call | flops 30198988800 | bytes 24903680 | tf_op jit(solution)/shard_map/pallas_call | solution.py:422
  90.7 2.0 %copy.11 = bf16[128,2560]{1,0:T(8,128)(2,1)} copy(bf16[128,2560]{1,0:T(8,128)(2,1)} %shard_map.91) | data formatting | bytes 1310720
